TPU v7x, 128 devices: a whole 4x4x4 slice. The times are simulated.
128 devices in a mesh: table: 32 (over z, x, core), code: 4 (over y).
Axes of the slice: x: 4, y: 4, z: 4, core: 2. Of those that a mesh axis runs over, the one named last changes fastest.
Arguments:
- pooled_grad: bfloat16 [32, 4, 2048, 128], P('table', 'code'), may hold values from -6 to 6
- bag_rows: int32 [32, 4, 32, 4, 2048], P('table', 'code'), may hold values from 0 to 511
- dest_blocks: int32 [32, 4, 32, 4], P('table', 'code'), may hold values from 0 to 95
- block_counts: int32 [32, 4, 32], P('table', 'code'), may hold values from 1 to 4, as said below
- table: float32 [32, 4, 96, 128, 128], P('table', 'code'), may hold values from -4 to 4
- accum: float32 [32, 4, 96, 128], P('table', 'code'), may hold values from 0.1 to 10
- parity: float32 [32, 96, 128, 128], P('table', 'code'), may hold values from -6 to 6
- parity_slot: int32 [32, 4, 96], P('table', 'code'), may hold values from 0 to 95, each once within a row
Outputs:
- new_table: float32 [32, 4, 96, 128, 128], P('table', 'code')
- new_accum: float32 [32, 4, 96, 128], P('table', 'code')
- new_parity: float32 [32, 96, 128, 128], P('table', 'code')
Inputs may be any that keep to these rules, and one draw needn't show every extreme that they name: `bag_rows`: A value r < 128 puts the sample into row r of the slot's block; larger values put it into none. `dest_blocks`: entries at slots k >= block_counts of that owner are ignored. Slots k >= block_counts[t, c, o] carry no block, and their entries of bag_rows and dest_blocks are ignored. For every index of the code axis some owner receives 4 blocks from every device of that index.
All inputs are finite; a program needn't handle non-finite values.
Results may differ from a plain program's by a relative error of at most 0.0015.
Values may be sent and summed in bfloat16 or wider, within the bound.
A program may use at most 128 MiB of HBM per device.

v0:
```python
import jax
import jax.numpy as jnp
from jax import lax
from jax.sharding import PartitionSpec as P

LEARN_RATE = 0.2


def body(pooled_grad, bag_rows, dest_blocks, block_counts, table, accum, parity, parity_slot):
    pooled = pooled_grad[0, 0]
    bag_lists = bag_rows[0, 0]
    dest_lists = dest_blocks[0, 0]
    counts = block_counts[0, 0]
    owners, capacity, batch_rows = bag_lists.shape
    blocks = table.shape[2]
    block_rows = table.shape[3]
    feature_width = table.shape[4]
    slot_total = owners * capacity
    group_size = 8
    live_mask = lax.broadcasted_iota(jnp.int32, (owners, capacity), 1) < counts[:, None]
    flat_bags = bag_lists.reshape(slot_total, batch_rows)
    flat_live = live_mask.reshape(slot_total)
    row_index = lax.broadcasted_iota(jnp.int32, (1, block_rows, 1), 1)

    def slot_terms(indices):
        group_bags = jnp.take(flat_bags, indices, axis=0)
        onehot = (group_bags[:, None, :] == row_index).astype(jnp.bfloat16)
        products = jnp.einsum("grs,se->gre", onehot, pooled, preferred_element_type=jnp.float32)
        keep_mask = jnp.take(flat_live, indices, axis=0)
        return jnp.where(keep_mask[:, None, None], products, 0.0).astype(jnp.bfloat16)

    indices = jnp.arange(slot_total, dtype=jnp.int32).reshape(slot_total // group_size, group_size)
    sent_rows = lax.map(slot_terms, indices).reshape(owners, capacity, block_rows, feature_width)
    marked = jnp.where(live_mask, dest_lists, blocks)
    received, received_ids = (
        lax.all_to_all(sent_rows, "table", split_axis=0, concat_axis=0, tiled=True),
        lax.all_to_all(marked, "table", split_axis=0, concat_axis=0, tiled=True),
    )
    block_index = lax.broadcasted_iota(jnp.int32, (blocks, 1), 0)
    selector = (received_ids.reshape(1, slot_total) == block_index).astype(jnp.bfloat16)
    summed_rows = jnp.dot(
        selector,
        received.reshape(slot_total, block_rows * feature_width),
        preferred_element_type=jnp.float32,
    )
    row_grad = summed_rows.astype(jnp.bfloat16).reshape(blocks, block_rows, feature_width)
    grad_float = row_grad.astype(jnp.float32)
    old_accum = accum[0, 0]
    new_accum = old_accum + jnp.mean(grad_float * grad_float, axis=-1)
    row_delta = -LEARN_RATE * grad_float * lax.rsqrt(new_accum)[:, :, None]
    new_table = table[0, 0] + row_delta
    position_order = jnp.argsort(parity_slot[0, 0])
    placed = jnp.take(row_delta, position_order, axis=0)
    parity_sum = lax.psum_scatter(placed, "code", scatter_dimension=0, tiled=True)
    new_parity = parity[0] + parity_sum
    return (new_table[None, None], new_accum[None, None], new_parity[None])


def solution(mesh):
    placed = (
        P("table", "code", None, None),
        P("table", "code", None, None, None),
        P("table", "code", None, None),
        P("table", "code", None),
        P("table", "code", None, None, None),
        P("table", "code", None, None),
        P("table", "code", None, None),
        P("table", "code", None),
    )
    return jax.shard_map(
        body,
        mesh=mesh,
        in_specs=placed,
        out_specs=(
            P("table", "code", None, None, None),
            P("table", "code", None, None),
            P("table", "code", None, None),
        ),
        check_vma=False,
    )
```

profile of v0, /device:TPU:1, one launch (start us, length us, event | category | flops | bytes accessed | tf_op | source)
XLA Modules:
  0.0 259.5 jit_solution(4515922447384279229)
XLA Ops:
  8.5 9.4 %all-to-all-start = ((s32[32,1,4]{2,1,0:T(1,128)}), s32[32,1,4]{2,1,0:T(1,128)S(1)}, u32[]{:S(2)}, u32[]{:S(2)}) async-start(s32[32,1,4]{2,1,0:T(1,128)} %copy.13), calls=%async_computation | async-start | bytes 32768 | tf_op jit(solution)/shard_map/all_to_all | solution.py:37
  19.6 83.5 %while.11 = (s32[]{:T(128)}, bf16[16,8,128,128]{3,2,1,0:T(8,128)(2,1)}, s32[16,8]{1,0:T(8,128)S(1)}, s32[128,2048]{1,0:T(8,128)S(1)}, bf16[2048,128]{1,0:T(8,128)(2,1)}, /*index=5*/s32[32]{0:T(128)}, s32[]{:T(128)}) while((s32[]{:T(128)}, bf16[16,8,128,128]{3,2,1,0:T(8,128)(2,1)}, s32[16,8]{1,0:T(8,128)S(1)}, ...), condition=%wide.region_1.2_spmd.clone, body=%wide.region_0.1_spmd.clone.sunk | while | flops 539247808 | bytes 1119065 | solution.py:33
  21.8 3.0 %fusion.28 = bf16[16,8,128,128]{3,2,1,0:T(8,128)(2,1)} fusion(bf16[16,8,128,128]{3,2,1,0:T(8,128)(2,1)} %get-tuple-element.122, s32[]{:T(128)S(6)} %copy.26, s32[8,2048]{1,0:T(8,128)S(1)} %broadcast_select_fusion.6, bf16[2048,128]{1,0:T(8,128)(2,1)} %get-tuple-element.132, pred[8]{0:T(512)(128)(4,1)S(1)} %get-tuple-element.113), kind=kOutput, calls=%fused_computation.11.clone.1 | convolution fusion | flops 539230208 | bytes 851980 | tf_op jit(solution)/shard_map/while/body/eval_jaxpr/grs,se->gre/dot_general | solution.py:28
  27.0 3.0 %fusion.28 = bf16[16,8,128,128]{3,2,1,0:T(8,128)(2,1)} fusion(bf16[16,8,128,128]{3,2,1,0:T(8,128)(2,1)} %get-tuple-element.122, s32[]{:T(128)S(6)} %copy.26, s32[8,2048]{1,0:T(8,128)S(1)} %broadcast_select_fusion.6, bf16[2048,128]{1,0:T(8,128)(2,1)} %get-tuple-element.132, pred[8]{0:T(512)(128)(4,1)S(1)} %get-tuple-element.113), kind=kOutput, calls=%fused_computation.11.clone.1 | convolution fusion | flops 539230208 | bytes 851980 | tf_op jit(solution)/shard_map/while/body/eval_jaxpr/grs,se->gre/dot_general | solution.py:28
  32.2 3.0 %fusion.28 = bf16[16,8,128,128]{3,2,1,0:T(8,128)(2,1)} fusion(bf16[16,8,128,128]{3,2,1,0:T(8,128)(2,1)} %get-tuple-element.122, s32[]{:T(128)S(6)} %copy.26, s32[8,2048]{1,0:T(8,128)S(1)} %broadcast_select_fusion.6, bf16[2048,128]{1,0:T(8,128)(2,1)} %get-tuple-element.132, pred[8]{0:T(512)(128)(4,1)S(1)} %get-tuple-element.113), kind=kOutput, calls=%fused_computation.11.clone.1 | convolution fusion | flops 539230208 | bytes 851980 | tf_op jit(solution)/shard_map/while/body/eval_jaxpr/grs,se->gre/dot_general | solution.py:28
  37.5 3.0 %fusion.28 = bf16[16,8,128,128]{3,2,1,0:T(8,128)(2,1)} fusion(bf16[16,8,128,128]{3,2,1,0:T(8,128)(2,1)} %get-tuple-element.122, s32[]{:T(128)S(6)} %copy.26, s32[8,2048]{1,0:T(8,128)S(1)} %broadcast_select_fusion.6, bf16[2048,128]{1,0:T(8,128)(2,1)} %get-tuple-element.132, pred[8]{0:T(512)(128)(4,1)S(1)} %get-tuple-element.113), kind=kOutput, calls=%fused_computation.11.clone.1 | convolution fusion | flops 539230208 | bytes 851980 | tf_op jit(solution)/shard_map/while/body/eval_jaxpr/grs,se->gre/dot_general | solution.py:28
  42.7 3.0 %fusion.28 = bf16[16,8,128,128]{3,2,1,0:T(8,128)(2,1)} fusion(bf16[16,8,128,128]{3,2,1,0:T(8,128)(2,1)} %get-tuple-element.122, s32[]{:T(128)S(6)} %copy.26, s32[8,2048]{1,0:T(8,128)S(1)} %broadcast_select_fusion.6, bf16[2048,128]{1,0:T(8,128)(2,1)} %get-tuple-element.132, pred[8]{0:T(512)(128)(4,1)S(1)} %get-tuple-element.113), kind=kOutput, calls=%fused_computation.11.clone.1 | convolution fusion | flops 539230208 | bytes 851980 | tf_op jit(solution)/shard_map/while/body/eval_jaxpr/grs,se->gre/dot_general | solution.py:28
  47.9 3.0 %fusion.28 = bf16[16,8,128,128]{3,2,1,0:T(8,128)(2,1)} fusion(bf16[16,8,128,128]{3,2,1,0:T(8,128)(2,1)} %get-tuple-element.122, s32[]{:T(128)S(6)} %copy.26, s32[8,2048]{1,0:T(8,128)S(1)} %broadcast_select_fusion.6, bf16[2048,128]{1,0:T(8,128)(2,1)} %get-tuple-element.132, pred[8]{0:T(512)(128)(4,1)S(1)} %get-tuple-element.113), kind=kOutput, calls=%fused_computation.11.clone.1 | convolution fusion | flops 539230208 | bytes 851980 | tf_op jit(solution)/shard_map/while/body/eval_jaxpr/grs,se->gre/dot_general | solution.py:28
  53.1 3.0 %fusion.28 = bf16[16,8,128,128]{3,2,1,0:T(8,128)(2,1)} fusion(bf16[16,8,128,128]{3,2,1,0:T(8,128)(2,1)} %get-tuple-element.122, s32[]{:T(128)S(6)} %copy.26, s32[8,2048]{1,0:T(8,128)S(1)} %broadcast_select_fusion.6, bf16[2048,128]{1,0:T(8,128)(2,1)} %get-tuple-element.132, pred[8]{0:T(512)(128)(4,1)S(1)} %get-tuple-element.113), kind=kOutput, calls=%fused_computation.11.clone.1 | convolution fusion | flops 539230208 | bytes 851980 | tf_op jit(solution)/shard_map/while/body/eval_jaxpr/grs,se->gre/dot_general | solution.py:28
  58.3 3.0 %fusion.28 = bf16[16,8,128,128]{3,2,1,0:T(8,128)(2,1)} fusion(bf16[16,8,128,128]{3,2,1,0:T(8,128)(2,1)} %get-tuple-element.122, s32[]{:T(128)S(6)} %copy.26, s32[8,2048]{1,0:T(8,128)S(1)} %broadcast_select_fusion.6, bf16[2048,128]{1,0:T(8,128)(2,1)} %get-tuple-element.132, pred[8]{0:T(512)(128)(4,1)S(1)} %get-tuple-element.113), kind=kOutput, calls=%fused_computation.11.clone.1 | convolution fusion | flops 539230208 | bytes 851980 | tf_op jit(solution)/shard_map/while/body/eval_jaxpr/grs,se->gre/dot_general | solution.py:28
  63.5 3.0 %fusion.28 = bf16[16,8,128,128]{3,2,1,0:T(8,128)(2,1)} fusion(bf16[16,8,128,128]{3,2,1,0:T(8,128)(2,1)} %get-tuple-element.122, s32[]{:T(128)S(6)} %copy.26, s32[8,2048]{1,0:T(8,128)S(1)} %broadcast_select_fusion.6, bf16[2048,128]{1,0:T(8,128)(2,1)} %get-tuple-element.132, pred[8]{0:T(512)(128)(4,1)S(1)} %get-tuple-element.113), kind=kOutput, calls=%fused_computation.11.clone.1 | convolution fusion | flops 539230208 | bytes 851980 | tf_op jit(solution)/shard_map/while/body/eval_jaxpr/grs,se->gre/dot_general | solution.py:28
  68.7 3.0 %fusion.28 = bf16[16,8,128,128]{3,2,1,0:T(8,128)(2,1)} fusion(bf16[16,8,128,128]{3,2,1,0:T(8,128)(2,1)} %get-tuple-element.122, s32[]{:T(128)S(6)} %copy.26, s32[8,2048]{1,0:T(8,128)S(1)} %broadcast_select_fusion.6, bf16[2048,128]{1,0:T(8,128)(2,1)} %get-tuple-element.132, pred[8]{0:T(512)(128)(4,1)S(1)} %get-tuple-element.113), kind=kOutput, calls=%fused_computation.11.clone.1 | convolution fusion | flops 539230208 | bytes 851980 | tf_op jit(solution)/shard_map/while/body/eval_jaxpr/grs,se->gre/dot_general | solution.py:28
  74.0 3.0 %fusion.28 = bf16[16,8,128,128]{3,2,1,0:T(8,128)(2,1)} fusion(bf16[16,8,128,128]{3,2,1,0:T(8,128)(2,1)} %get-tuple-element.122, s32[]{:T(128)S(6)} %copy.26, s32[8,2048]{1,0:T(8,128)S(1)} %broadcast_select_fusion.6, bf16[2048,128]{1,0:T(8,128)(2,1)} %get-tuple-element.132, pred[8]{0:T(512)(128)(4,1)S(1)} %get-tuple-element.113), kind=kOutput, calls=%fused_computation.11.clone.1 | convolution fusion | flops 539230208 | bytes 851980 | tf_op jit(solution)/shard_map/while/body/eval_jaxpr/grs,se->gre/dot_general | solution.py:28
  79.2 3.0 %fusion.28 = bf16[16,8,128,128]{3,2,1,0:T(8,128)(2,1)} fusion(bf16[16,8,128,128]{3,2,1,0:T(8,128)(2,1)} %get-tuple-element.122, s32[]{:T(128)S(6)} %copy.26, s32[8,2048]{1,0:T(8,128)S(1)} %broadcast_select_fusion.6, bf16[2048,128]{1,0:T(8,128)(2,1)} %get-tuple-element.132, pred[8]{0:T(512)(128)(4,1)S(1)} %get-tuple-element.113), kind=kOutput, calls=%fused_computation.11.clone.1 | convolution fusion | flops 539230208 | bytes 851980 | tf_op jit(solution)/shard_map/while/body/eval_jaxpr/grs,se->gre/dot_general | solution.py:28
  84.4 3.0 %fusion.28 = bf16[16,8,128,128]{3,2,1,0:T(8,128)(2,1)} fusion(bf16[16,8,128,128]{3,2,1,0:T(8,128)(2,1)} %get-tuple-element.122, s32[]{:T(128)S(6)} %copy.26, s32[8,2048]{1,0:T(8,128)S(1)} %broadcast_select_fusion.6, bf16[2048,128]{1,0:T(8,128)(2,1)} %get-tuple-element.132, pred[8]{0:T(512)(128)(4,1)S(1)} %get-tuple-element.113), kind=kOutput, calls=%fused_computation.11.clone.1 | convolution fusion | flops 539230208 | bytes 851980 | tf_op jit(solution)/shard_map/while/body/eval_jaxpr/grs,se->gre/dot_general | solution.py:28
  100.0 3.0 %fusion.28 = bf16[16,8,128,128]{3,2,1,0:T(8,128)(2,1)} fusion(bf16[16,8,128,128]{3,2,1,0:T(8,128)(2,1)} %get-tuple-element.122, s32[]{:T(128)S(6)} %copy.26, s32[8,2048]{1,0:T(8,128)S(1)} %broadcast_select_fusion.6, bf16[2048,128]{1,0:T(8,128)(2,1)} %get-tuple-element.132, pred[8]{0:T(512)(128)(4,1)S(1)} %get-tuple-element.113), kind=kOutput, calls=%fused_computation.11.clone.1 | convolution fusion | flops 539230208 | bytes 851980 | tf_op jit(solution)/shard_map/while/body/eval_jaxpr/grs,se->gre/dot_general | solution.py:28
  103.1 7.6 %all-to-all-start.1 = ((bf16[32,4,128,128]{3,2,1,0:T(8,128)(2,1)}), bf16[32,4,128,128]{3,2,1,0:T(8,128)(2,1)}, u32[]{:S(2)}, u32[]{:S(2)}) async-start(bf16[32,4,128,128]{3,2,1,0:T(8,128)(2,1)} %bitcast.60), calls=%async_computation.1 | async-start | bytes 8388608 | tf_op jit(solution)/shard_map/all_to_all | solution.py:36
  114.6 46.3 %all-to-all-done.1 = bf16[32,4,128,128]{3,2,1,0:T(8,128)(2,1)} async-done(((bf16[32,4,128,128]{3,2,1,0:T(8,128)(2,1)}), bf16[32,4,128,128]{3,2,1,0:T(8,128)(2,1)}, u32[]{:S(2)}, u32[]{:S(2)}) %all-to-all-start.1) | async-done | bytes 4194336 | tf_op jit(solution)/shard_map/all_to_all | solution.py:36
  160.9 5.1 %fusion.16 = f32[12,8,128,128]{3,1,2,0:T(8,128)S(1)} fusion(bf16[16,8,128,128]{3,2,1,0:T(8,128)(2,1)} %bitcast.15, s32[128]{0:T(128)S(1)} %eq.30), kind=kOutput, calls=%fused_computation.31 | convolution fusion | flops 405811200 | bytes 10486272 | tf_op jit(solution)/shard_map/dot_general | solution.py:41
  169.8 3.8 %bitcast_multiply_fusion = f32[96,128,128]{2,1,0:T(8,128)} fusion(f32[12,8,128,128]{3,2,1,0:T(8,128)S(1)} %copy.15, f32[96,128]{1,0:T(8,128)S(1)} %fusion.21), kind=kLoop, calls=%fused_computation.24 | loop fusion | flops 1572864 | bytes 12632064 | tf_op jit(solution)/shard_map/mul | solution.py:50
  173.6 6.4 %gather_fusion.2 = f32[96,128,128]{2,1,0:T(8,128)} fusion(f32[96,128,128]{2,1,0:T(8,128)} %bitcast_multiply_fusion, s32[1024]{0:T(1024)S(1)} %pad_clamp_fusion.1), kind=kCustom, calls=%fused_computation.2 | custom fusion | bytes 12583296 | tf_op jit(solution)/shard_map/jit(_take)/gather | solution.py:53
  180.0 5.9 %broadcast_select_fusion.2 = f32[96,128,128]{2,1,0:T(8,128)} fusion(f32[96,128,128]{2,1,0:T(8,128)} %gather_fusion.2, pred[96]{0:T(512)(128)(4,1)S(1)} %compare_and_fusion.1), kind=kLoop, calls=%fused_computation.30 | loop fusion | flops 1572864 | bytes 12583008 | tf_op jit(solution)/shard_map/jit(_take)/select_n | solution.py:53
  186.5 9.0 %multiply_add_fusion = f32[1,1,96,128,128]{4,3,2,1,0:T(8,128)} fusion(f32[1,1,96,128,128]{4,3,2,1,0:T(8,128)} %param.14, f32[1,1,96,128,128]{4,3,2,1,0:T(8,128)} %bitcast.59, f32[96,128]{1,0:T(8,128)S(1)} %fusion.21), kind=kLoop, calls=%fused_computation.27 | loop fusion | flops 3145728 | bytes 18923520 | tf_op jit(solution)/shard_map/add | solution.py:51
  195.6 54.3 %reduce-scatter.2.cloned.1.call-done = f32[24,128,128]{2,1,0:T(8,128)} async-done(((f32[96,128,128]{2,1,0:T(8,128)}), f32[24,128,128]{2,1,0:T(8,128)}) %reduce-scatter.2.cloned.1.call-update) | async-done | bytes 1572880 | tf_op jit(solution)/shard_map/reduce_scatter | solution.py:54
  (159 shorter events, 54.9 us)
Async XLA Ops:
  8.5 94.5 %all-to-all-start = ((s32[32,1,4]{2,1,0:T(1,128)}), s32[32,1,4]{2,1,0:T(1,128)S(1)}, u32[]{:S(2)}, u32[]{:S(2)}) async-start(s32[32,1,4]{2,1,0:T(1,128)} %copy.13), calls=%async_computation | async-start | bytes 32768 | tf_op jit(solution)/shard_map/all_to_all | solution.py:37
  103.1 7.6 %copy-start.3 = (s32[1,1,96]{2,1,0:T(1,128)S(1)}, s32[1,1,96]{2,1,0:T(1,128)}, u32[]{:S(2)}) copy-start(s32[1,1,96]{2,1,0:T(1,128)} %param.17) | copy-start | bytes 1156
  103.1 57.8 %all-to-all-start.1 = ((bf16[32,4,128,128]{3,2,1,0:T(8,128)(2,1)}), bf16[32,4,128,128]{3,2,1,0:T(8,128)(2,1)}, u32[]{:S(2)}, u32[]{:S(2)}) async-start(bf16[32,4,128,128]{3,2,1,0:T(8,128)(2,1)} %bitcast.60), calls=%async_computation.1 | async-start | bytes 8388608 | tf_op jit(solution)/shard_map/all_to_all | solution.py:36
  110.6 139.3 %reduce-scatter.2.cloned.1.call-start = ((), (), s32[]{:S(2)}) async-start(), calls=%async_computation.3 | async-start | bytes 7864320 | tf_op jit(solution)/shard_map/reduce_scatter | solution.py:54
  167.1 2.7 %copy-start = (f32[12,8,128,128]{3,2,1,0:T(8,128)}, f32[12,8,128,128]{3,2,1,0:T(8,128)S(1)}, u32[]{:S(2)}) copy-start(f32[12,8,128,128]{3,2,1,0:T(8,128)S(1)} %copy.15) | copy-start | bytes 18874372
  167.1 1.7 copy-start.2
  186.5 63.4 %copy-start.1 = (f32[1,24,128,128]{3,2,1,0:T(8,128)S(1)}, f32[1,24,128,128]{3,2,1,0:T(8,128)}, u32[]{:S(2)}) copy-start(f32[1,24,128,128]{3,2,1,0:T(8,128)} %param.16) | copy-start | bytes 4718596
Sparse Core Ops, SparseCore 0:
  186.0 63.8 reduce-scatter.1
where the time goes:
time: 261 us; the launch traced here: 259 us
  waiting for transfers between devices  101 us (39%)
  matrix products  53.5 us (20%)
  other arithmetic  41.2 us (16%)
  local copies, waits for them, and re-layouts  32.7 us (13%)
  starting transfers between devices  17 us (7%)
  between operations  14.2 us (5%)
    reduce_scatter x1, waiting for transfers between devices, body(): lax.psum_scatter(placed, 'code', scatter_dimension=0, tiled=True)  54.3 us
    dot_general x16, matrix products, slot_terms(): jnp.einsum('grs,se->gre', onehot, pooled, preferred_element_type=jnp.floa...  48.4 us
    all_to_all x1, waiting for transfers between devices, body(): lax.all_to_all(sent_rows, 'table', split_axis=0, concat_axis=0, tiled=True)  46.3 us
    lt x16, other arithmetic, body(): lax.broadcasted_iota(jnp.int32, (owners, capacity), 1) < counts[:, None]  11.7 us
    gather x16, local copies, waits for them, and re-layouts, slot_terms(): keep_mask = jnp.take(flat_live, indices, axis=0)  10.4 us
    all_to_all x1, starting transfers between devices, body(): lax.all_to_all(marked, 'table', split_axis=0, concat_axis=0, tiled=True)  9.43 us
    gather x16, local copies, waits for them, and re-layouts, slot_terms(): group_bags = jnp.take(flat_bags, indices, axis=0)  9.21 us
    add x1, other arithmetic, body(): new_table = table[0, 0] + row_delta  9.04 us
  transfers between devices with their start and end apart: 3, of which 2 were waited for; matrix products, arithmetic and copies ran while one was open for 38% of the time, Pallas kernels for 0%

commit v1 on v0

v1 whole, which is shorter than its diff:
```python
import jax
import jax.numpy as jnp
from jax import lax
from jax.experimental import pallas as pl
from jax.experimental.pallas import tpu as pltpu
from jax.sharding import PartitionSpec as P

LEARN_RATE = 0.2
MESH = pl.DeviceIdType.MESH

RING = 4
CORES = 2
OWNERS = RING * RING * CORES
CODERS = 4
CAP = 4
E = 128
BLK = 128
BLOCKS = 96
HELD = BLOCKS // CODERS
BATCH = 2048

ROWS = 16
CHUNKS = BLK // ROWS
GROUP = 8
PARITY_GROUP = 32
LAG = 3
SLOT_ROWS = CAP * ROWS
PAIRS = OWNERS // 2


def send_order():
    offsets = [(dz, dx, dc) for dz in range(RING) for dx in range(RING) for dc in range(CORES)][1:]
    offsets.sort(key=lambda m: -(min(m[0], RING - m[0]) + min(m[1], RING - m[1])))
    order = []
    for dz, dx, dc in offsets:
        for _ in range(4):
            if (dz, dx, dc) not in order:
                order.append((dz, dx, dc))
            dz, dx = dx, (RING - dz) % RING
    return order


ORDER = send_order()
PEERS = len(ORDER)


def kernel(
    pooled_hbm, bags_hbm, dest_ref, count_ref, table_hbm, accum_ref, parity_hbm, slot_ref,
    table_out, accum_out, parity_out,
    pooled, bags, id_send, id_recv, sent, received, selector, table, parity, accum_t, new_accum_t,
    delta, delta_send, delta_recv,
    in_sem, id_send_sem, id_recv_sem, send_sem, recv_sem, own_sem, delta_send_sem, delta_recv_sem,
    table_sem, parity_sem,
):
    me = lax.axis_index("table")
    code = lax.axis_index("code")
    z, x, core = me // (RING * CORES), (me // CORES) % RING, me % CORES

    def owner_at(offset):
        dz, dx, dc = offset
        return (((z + dz) % RING) * RING + (x + dx) % RING) * CORES + (core + dc) % CORES

    barrier = pltpu.get_barrier_semaphore()
    for offset in ORDER:
        pl.semaphore_signal(barrier, inc=1, device_id=(owner_at(offset), code), device_id_type=MESH)
    for step in range(1, CODERS):
        pl.semaphore_signal(barrier, inc=1, device_id=(me, (code + step) % CODERS), device_id_type=MESH)

    loads = [
        pltpu.make_async_copy(pooled_hbm, pooled, in_sem.at[0]),
        pltpu.make_async_copy(bags_hbm, bags, in_sem.at[1]),
        pltpu.make_async_copy(table_hbm, table, in_sem.at[2]),
        pltpu.make_async_copy(parity_hbm, parity, in_sem.at[3]),
    ]
    for load in loads:
        load.start()

    lane = lax.broadcasted_iota(jnp.int32, (1, E), 1)
    lane_slot = (lane // ROWS) % CAP
    for owner in range(OWNERS):
        ids = jnp.full((1, E), -1, jnp.int32)
        for k in range(CAP):
            ids = jnp.where((lane_slot == k) & (k < count_ref[0, owner]), dest_ref[k, owner], ids)
        id_send[owner] = ids

    slot_lanes = jnp.full((1, E), -1, jnp.int32)
    for b in range(BLOCKS):
        slot_lanes = jnp.where(lane == b, slot_ref[0, b], slot_lanes)

    padding = jnp.zeros((BLK - BLOCKS, BLK), jnp.float32)
    accum_t[...] = jnp.concatenate([accum_ref[...], padding], axis=0).T
    new_accum_t[...] = jnp.zeros_like(new_accum_t)

    loads[0].wait()
    loads[1].wait()

    def slot_terms(q):
        row_index = lax.broadcasted_iota(jnp.int32, (ROWS, E), 0) + q * ROWS

        def group_terms(g, carry):
            tiles = []
            for j in range(GROUP):
                owner = g * GROUP + j
                for k in range(CAP):
                    wanted = jnp.where(k < count_ref[0, owner], row_index, -1)
                    wanted = jnp.concatenate([wanted] * (BATCH // E), axis=1)
                    bag = bags[owner, pl.ds(k, 1), :]
                    tiles.append(jnp.where(bag == wanted, 1.0, 0.0).astype(jnp.bfloat16))
            onehot = jnp.concatenate(tiles, axis=0)
            sums = jnp.dot(onehot, pooled[...], preferred_element_type=jnp.float32)
            sent[q, pl.ds(g * GROUP, GROUP)] = sums.astype(jnp.bfloat16).reshape(GROUP, SLOT_ROWS, E)
            return carry

        lax.fori_loop(0, OWNERS // GROUP, group_terms, 0)

    def send_ids():
        for i, offset in enumerate(ORDER):
            owner = owner_at(offset)
            pltpu.make_async_remote_copy(
                src_ref=id_send.at[owner], dst_ref=id_recv.at[i],
                send_sem=id_send_sem, recv_sem=id_recv_sem,
                device_id=(owner, code), device_id_type=MESH,
            ).start()

    def send_chunk(q):
        for i, offset in enumerate(ORDER):
            owner = owner_at(offset)
            pltpu.make_async_remote_copy(
                src_ref=sent.at[q, owner], dst_ref=received.at[q, i],
                send_sem=send_sem.at[q], recv_sem=recv_sem.at[q],
                device_id=(owner, code), device_id_type=MESH,
            ).start()
        pltpu.make_async_copy(sent.at[q, me], received.at[q, PEERS], own_sem.at[q]).start()

    def all_ids():
        return pltpu.make_async_remote_copy(
            src_ref=id_send.at[pl.ds(0, PEERS)], dst_ref=id_recv.at[pl.ds(0, PEERS)],
            send_sem=id_send_sem, recv_sem=id_recv_sem, device_id=(me, code), device_id_type=MESH,
        )

    def whole_chunk(q):
        return pltpu.make_async_remote_copy(
            src_ref=sent.at[q, pl.ds(0, PEERS)], dst_ref=received.at[q, pl.ds(0, PEERS)],
            send_sem=send_sem.at[q], recv_sem=recv_sem.at[q], device_id=(me, code), device_id_type=MESH,
        )

    def build_selector():
        all_ids().wait_recv()
        ids = jnp.concatenate([id_recv[i] for i in range(PEERS)] + [id_send[me]], axis=0)
        row_in_chunk = lax.broadcasted_iota(jnp.int32, (OWNERS, E), 1) % ROWS
        keys = jnp.full((OWNERS, E), -1, jnp.int32)
        for b in range(BLOCKS):
            keys = jnp.where(ids == b, slot_ref[0, b] * ROWS + row_in_chunk, keys)
        pairs = []
        for i in range(PAIRS):
            low, high = keys[2 * i : 2 * i + 1, :], keys[2 * i + 1 : 2 * i + 2, :]
            pairs.append(jnp.broadcast_to(jnp.where(lane < SLOT_ROWS, low, high), (ROWS, E)))
        row_index = lax.broadcasted_iota(jnp.int32, (ROWS, E), 0)

        def selector_rows(p, carry):
            wanted = row_index + p * ROWS
            tiles = [jnp.where(pair == wanted, 1.0, 0.0).astype(jnp.bfloat16) for pair in pairs]
            selector[pl.ds(pl.multiple_of(p * ROWS, ROWS), ROWS), :] = jnp.concatenate(tiles, axis=1)
            return carry

        lax.fori_loop(0, BLOCKS, selector_rows, 0)

    def delta_copies(q):
        copies = []
        for step in range(1, CODERS):
            holder = (code + step) % CODERS
            copies.append(
                pltpu.make_async_remote_copy(
                    src_ref=delta_send.at[q, pl.ds(holder * HELD, HELD)], dst_ref=delta_recv.at[q, step - 1],
                    send_sem=delta_send_sem.at[q], recv_sem=delta_recv_sem.at[q],
                    device_id=(me, holder), device_id_type=MESH,
                )
            )
        return copies

    def all_deltas(q):
        span = pl.ds(0, (CODERS - 1) * HELD)
        return pltpu.make_async_remote_copy(
            src_ref=delta_send.at[q, span], dst_ref=delta_send.at[q, span],
            send_sem=delta_send_sem.at[q], recv_sem=delta_recv_sem.at[q], device_id=(me, code), device_id_type=MESH,
        )

    def table_copy(q):
        rows = pl.ds(pl.multiple_of(q * ROWS, ROWS), ROWS)
        return pltpu.make_async_copy(table.at[:, rows, :], table_out.at[:, rows, :], table_sem.at[q])

    def parity_copy(q):
        rows = pl.ds(pl.multiple_of(q * ROWS, ROWS), ROWS)
        return pltpu.make_async_copy(parity.at[:, rows, :], parity_out.at[:, rows, :], parity_sem.at[q])

    def combine(q):
        rows = pl.ds(pl.multiple_of(q * ROWS, ROWS), ROWS)
        whole_chunk(q).wait_recv()
        pltpu.make_async_copy(sent.at[q, me], received.at[q, PEERS], own_sem.at[q]).wait()
        terms = received[q].reshape(OWNERS * SLOT_ROWS, E)
        old = accum_t[rows, :]

        def block_group(m, carry):
            first = pl.multiple_of(m * (PARITY_GROUP * ROWS), PARITY_GROUP * ROWS)
            sums = jnp.dot(selector[pl.ds(first, PARITY_GROUP * ROWS), :], terms, preferred_element_type=jnp.float32)
            grad = sums.astype(jnp.bfloat16).astype(jnp.float32).reshape(PARITY_GROUP, ROWS, E)
            block = lax.broadcasted_iota(jnp.int32, (PARITY_GROUP, ROWS, E), 0) + m * PARITY_GROUP
            mine = slot_lanes.reshape(1, 1, E) == block
            accum = jnp.sum(jnp.where(mine, old[None], 0.0), axis=-1, keepdims=True)
            accum = accum + jnp.sum(grad * grad, axis=-1, keepdims=True) * (1.0 / E)
            change = grad * (-LEARN_RATE * lax.rsqrt(accum))
            delta[pl.ds(m * PARITY_GROUP, PARITY_GROUP)] = change
            delta_send[q, pl.ds(m * PARITY_GROUP, PARITY_GROUP)] = change.astype(jnp.bfloat16)
            new_accum_t[rows, :] += jnp.sum(jnp.where(mine, accum, 0.0), axis=0)
            return carry

        lax.fori_loop(0, BLOCKS // PARITY_GROUP, block_group, 0)
        for copy in delta_copies(q):
            copy.start()

        def add_block(i, carry):
            for j in range(8):
                b = i * 8 + j
                table[b, rows, :] += delta[slot_ref[0, b]]
            return carry

        lax.fori_loop(0, BLOCKS // 8, add_block, 0)
        table_copy(q).start()
        parity[:, rows, :] += delta[pl.ds(code * HELD, HELD)]

    def finish(q):
        rows = pl.ds(pl.multiple_of(q * ROWS, ROWS), ROWS)
        all_deltas(q).wait_recv()
        total = parity[:, rows, :]
        for j in range(CODERS - 1):
            total += delta_recv[q, j].astype(jnp.float32)
        parity[:, rows, :] = total
        parity_copy(q).start()

    def step(s, carry):
        @pl.when(s < CHUNKS)
        def _():
            slot_terms(s)

        @pl.when(s == 0)
        def _():
            pl.semaphore_wait(barrier, PEERS + CODERS - 1)
            send_ids()

        @pl.when(s < CHUNKS)
        def _():
            send_chunk(s)

        @pl.when(s == 1)
        def _():
            build_selector()

        @pl.when(s == LAG)
        def _():
            loads[2].wait()
            loads[3].wait()

        @pl.when((s >= LAG) & (s < CHUNKS + LAG))
        def _():
            combine(s - LAG)

        @pl.when(s >= LAG + 2)
        def _():
            finish(s - LAG - 2)

        return carry

    lax.fori_loop(0, CHUNKS + LAG + 2, step, 0)
    accum_out[...] = new_accum_t[...].T[:BLOCKS, :]

    all_ids().wait_send()

    def drain(q, carry):
        whole_chunk(q).wait_send()
        all_deltas(q).wait_send()
        table_copy(q).wait()
        parity_copy(q).wait()
        return carry

    lax.fori_loop(0, CHUNKS, drain, 0)


def body(pooled_grad, bag_rows, dest_blocks, block_counts, table, accum, parity, parity_slot):
    anywhere = pl.BlockSpec(memory_space=pl.ANY)
    vmem = pl.BlockSpec(memory_space=pltpu.VMEM)
    smem = pl.BlockSpec(memory_space=pltpu.SMEM)
    dma = pltpu.SemaphoreType.DMA
    f32, bf16, i32 = jnp.float32, jnp.bfloat16, jnp.int32
    new_table, new_accum, new_parity = pl.pallas_call(
        kernel,
        name="adagrad_step",
        out_shape=(
            jax.ShapeDtypeStruct((BLOCKS, BLK, E), f32),
            jax.ShapeDtypeStruct((BLOCKS, BLK), f32),
            jax.ShapeDtypeStruct((HELD, BLK, E), f32),
        ),
        in_specs=[anywhere, anywhere, smem, smem, anywhere, vmem, anywhere, smem],
        out_specs=(anywhere, vmem, anywhere),
        scratch_shapes=[
            pltpu.VMEM((BATCH, E), bf16),
            pltpu.VMEM((OWNERS, CAP, BATCH), i32),
            pltpu.VMEM((OWNERS, 1, E), i32),
            pltpu.VMEM((PEERS, 1, E), i32),
            pltpu.VMEM((CHUNKS, OWNERS, SLOT_ROWS, E), bf16),
            pltpu.VMEM((CHUNKS, OWNERS, SLOT_ROWS, E), bf16),
            pltpu.VMEM((BLOCKS * ROWS, OWNERS * SLOT_ROWS), bf16),
            pltpu.VMEM((BLOCKS, BLK, E), f32),
            pltpu.VMEM((HELD, BLK, E), f32),
            pltpu.VMEM((BLK, BLK), f32),
            pltpu.VMEM((BLK, BLK), f32),
            pltpu.VMEM((BLOCKS, ROWS, E), f32),
            pltpu.VMEM((CHUNKS, BLOCKS, ROWS, E), bf16),
            pltpu.VMEM((CHUNKS, CODERS - 1, HELD, ROWS, E), bf16),
            dma((4,)),
            dma,
            dma,
            dma((CHUNKS,)),
            dma((CHUNKS,)),
            dma((CHUNKS,)),
            dma((CHUNKS,)),
            dma((CHUNKS,)),
            dma((CHUNKS,)),
            dma((CHUNKS,)),
        ],
        compiler_params=pltpu.CompilerParams(
            collective_id=0, has_side_effects=True, vmem_limit_bytes=56 * 1024 * 1024
        ),
    )(
        pooled_grad[0, 0], bag_rows[0, 0], dest_blocks[0, 0].T, block_counts[0],
        table[0, 0], accum[0, 0], parity[0], parity_slot[0],
    )
    return (new_table[None, None], new_accum[None, None], new_parity[None])


def solution(mesh):
    placed = (
        P("table", "code", None, None),
        P("table", "code", None, None, None),
        P("table", "code", None, None),
        P("table", "code", None),
        P("table", "code", None, None, None),
        P("table", "code", None, None),
        P("table", "code", None, None),
        P("table", "code", None),
    )
    return jax.shard_map(
        body,
        mesh=mesh,
        in_specs=placed,
        out_specs=(
            P("table", "code", None, None, None),
            P("table", "code", None, None),
            P("table", "code", None, None),
        ),
        check_vma=False,
    )
```

time: 261 us -> 79.5 us (0.30)
  waiting for transfers between devices: 101 us -> 0 us
  Pallas kernels: 0 us -> 70.5 us
  matrix products: 53.5 us -> 0 us
  other arithmetic: 41.2 us -> 0 us
  local copies, waits for them, and re-layouts: 32.7 us -> 8.18 us
  starting transfers between devices: 17 us -> 0 us
  between operations: 14.2 us -> 0.66 us
    pallas_call x0 -> x1, Pallas kernels: none -> 70.5 us  [body(): pl.pallas_call(kernel, name='adagrad_step', out_shape=(jax.ShapeDtypeStru...]
    reduce_scatter x1 -> x0, waiting for transfers between devices: 54.3 us -> none  [body(): lax.psum_scatter(placed, 'code', scatter_dimension=0, tiled=True)]
    dot_general x17 -> x0, matrix products: 53.5 us -> none  [the longest x16 48.4 us: slot_terms(): jnp.einsum('grs,se->gre', onehot, pooled, preferred_element_type=jnp.floa...]
    all_to_all x2 -> x0, waiting for transfers between devices: 46.3 us -> none  [the longest x1 46.3 us: body(): lax.all_to_all(sent_rows, 'table', split_axis=0, concat_axis=0, tiled=True)]
    gather x33 -> x0, local copies, waits for them, and re-layouts: 26 us -> none  [the longest x16 10.4 us: slot_terms(): keep_mask = jnp.take(flat_live, indices, axis=0)]
    all_to_all x2 -> x0, starting transfers between devices: 17 us -> none  [the longest x1 9.43 us: body(): lax.all_to_all(marked, 'table', split_axis=0, concat_axis=0, tiled=True)]
    lt x16 -> x0, other arithmetic: 11.7 us -> none  [body(): lax.broadcasted_iota(jnp.int32, (owners, capacity), 1) < counts[:, None]]
    add x2 -> x0, other arithmetic: 9.67 us -> none  [the longest x1 9.04 us: body(): new_table = table[0, 0] + row_delta]
  transfers between devices with their start and end apart: 3 -> 0, of which waited for: 2 -> 0; matrix products, arithmetic and copies ran while one was open for 38% -> 0% of each run, Pallas kernels for 0% -> 0%
where the time goes in v1:
time: 79.5 us; the launch traced here: 79.4 us
  Pallas kernels  70.5 us (89%)
  local copies, waits for them, and re-layouts  8.18 us (10%)
    pallas_call x1, Pallas kernels, body(): pl.pallas_call(kernel, name='adagrad_step', out_shape=(jax.ShapeDtypeStru...  70.5 us
    unnamed x7, local copies, waits for them, and re-layouts  8.18 us

profile of v1, /device:TPU:1, one launch (start us, length us, event | category | flops | bytes accessed | tf_op | source)
XLA Modules:
  0.0 79.4 jit_solution(2390466992511269007)
XLA Ops:
  0.6 70.5 %adagrad_step.1 = (f32[96,128,128]{2,1,0:T(8,128)}, f32[96,128]{1,0:T(8,128)}, f32[24,128,128]{2,1,0:T(8,128)}) custom-call(bf16[2048,128]{1,0:T(8,128)(2,1)} %bitcast.18, s32[32,4,2048]{2,1,0:T(4,128)} %bitcast.17, s32[4,32]{1,0:T(4,128)} %bitcast.21, s32[1,32]{1,0:T(1,128)} %bitcast.22, f32[96,128,128]{2,1,0:T(8,128)} %bitcast.14, f32[96,128]{1,0:T(8,128)} %bitcast.19, ...), custom_call_target="tpu_custom_call" | custom-call | tf_op jit(solution)/shard_map/adagrad_step/pallas_call | solution.py:294
  71.2 0.0 copy-start.1
  71.2 0.0 copy-start
  71.2 6.4 %copy.14 = f32[1,1,96,128,128]{4,3,2,1,0:T(8,128)} copy(f32[1,1,96,128,128]{4,3,2,1,0:T(8,128)} %bitcast.13) | data formatting | bytes 12582912
  77.6 0.0 copy-done.1
  77.6 0.6 copy.15
  78.2 0.0 copy-done
  78.2 1.1 %copy.16 = f32[1,24,128,128]{3,2,1,0:T(8,128)} copy(f32[1,24,128,128]{3,2,1,0:T(8,128)S(1)} %bitcast.15) | data formatting | bytes 3145728
Async XLA Ops:
  71.2 6.4 %copy-start.1 = (f32[96,128]{1,0:T(8,128)S(1)}, f32[96,128]{1,0:T(8,128)}, u32[]{:S(2)}) copy-start(f32[96,128]{1,0:T(8,128)} %get-tuple-element.7) | copy-start | bytes 147460
  71.2 7.0 %copy-start = (f32[24,128,128]{2,1,0:T(8,128)S(1)}, f32[24,128,128]{2,1,0:T(8,128)}, u32[]{:S(2)}) copy-start(f32[24,128,128]{2,1,0:T(8,128)} %get-tuple-element.8) | copy-start | bytes 4718596

commit v2 on v0

v2 whole, which is shorter than its diff:
```python
import jax
import jax.numpy as jnp
from jax import lax
from jax.experimental import pallas as pl
from jax.experimental.pallas import tpu as pltpu
from jax.sharding import PartitionSpec as P

LEARN_RATE = 0.2
MESH = pl.DeviceIdType.MESH

RING = 4
CORES = 2
OWNERS = RING * RING * CORES
CODERS = 4
CAP = 4
E = 128
BLK = 128
BLOCKS = 96
HELD = BLOCKS // CODERS
BATCH = 2048

UNIT = 8
UNITS = BLK // UNIT
UNIT_TERMS = CAP * UNIT
WIDE_UNITS, WIDE_CHUNKS = 2, 7
THIN_UNITS, THIN_CHUNKS = 1, 2
DOT_ROWS = 512
LAG = 2


def send_order():
    offsets = [(dz, dx, dc) for dz in range(RING) for dx in range(RING) for dc in range(CORES)][1:]
    offsets.sort(key=lambda m: -(min(m[0], RING - m[0]) + min(m[1], RING - m[1])))
    order = []
    for dz, dx, dc in offsets:
        for _ in range(4):
            if (dz, dx, dc) not in order:
                order.append((dz, dx, dc))
            dz, dx = dx, (RING - dz) % RING
    return order


ORDER = send_order()
PEERS = len(ORDER)


class Stage:
    def __init__(self, units, first_unit, first_chunk, chunks, env, scratch):
        self.units, self.first_unit, self.first_chunk, self.chunks = units, first_unit, first_chunk, chunks
        self.env = env
        self.sent, self.received, self.send_sem, self.recv_sem = scratch

    @staticmethod
    def scratch_shapes(units, chunks):
        bf16, dma = jnp.bfloat16, pltpu.SemaphoreType.DMA
        return [
            pltpu.VMEM((chunks, PEERS, units * UNIT_TERMS, E), bf16),
            pltpu.VMEM((chunks, OWNERS, units * UNIT_TERMS, E), bf16),
            dma((chunks,)),
            dma((chunks,)),
        ]

    def send_terms(self, q, before_first_send=None):
        env = self.env
        terms = self.units * UNIT_TERMS
        row_index = lax.broadcasted_iota(jnp.int32, (UNIT, E), 0) + (self.first_unit + q * self.units) * UNIT
        group = DOT_ROWS // terms
        for start in range(0, OWNERS, group):
            tiles, part = [], []
            for i in range(start, start + group):
                owner = env.owners[i]
                for h in range(self.units):
                    for k in range(CAP):
                        wanted = jnp.where(k < env.counts[0, owner], row_index + h * UNIT, -1)
                        wanted = jnp.concatenate([wanted] * (BATCH // E), axis=1)
                        part.append(jnp.where(env.bags[owner, pl.ds(k, 1), :] == wanted, 1.0, 0.0))
                        if len(part) == 2:
                            tiles.append(jnp.concatenate(part, axis=0).astype(jnp.bfloat16))
                            part = []
            onehot = jnp.concatenate(tiles, axis=0)
            sums = jnp.dot(onehot, env.pooled[...], preferred_element_type=jnp.float32)
            sums = sums.astype(jnp.bfloat16).reshape(group, terms, E)
            if start + group < OWNERS:
                self.sent[q, pl.ds(start, group)] = sums
            else:
                self.sent[q, pl.ds(start, group - 1)] = sums[: group - 1]
                self.received[q, PEERS] = sums[group - 1]
        if before_first_send is not None:
            before_first_send()
        for i in range(PEERS):
            pltpu.make_async_remote_copy(
                src_ref=self.sent.at[q, i], dst_ref=self.received.at[q, i],
                send_sem=self.send_sem.at[q], recv_sem=self.recv_sem.at[q],
                device_id=(env.owners[i], env.code), device_id_type=MESH,
            ).start()

    def all_terms(self, q):
        return pltpu.make_async_remote_copy(
            src_ref=self.sent.at[q], dst_ref=self.received.at[q, pl.ds(0, PEERS)],
            send_sem=self.send_sem.at[q], recv_sem=self.recv_sem.at[q],
            device_id=(self.env.me, self.env.code), device_id_type=MESH,
        )

    def combine(self, q):
        env = self.env
        self.all_terms(q).wait_recv()

        def combine_unit(h, carry):
            unit = self.first_unit + q * self.units + h
            first = pl.multiple_of(h * UNIT_TERMS, UNIT_TERMS)
            env.combine_unit(unit, h, self.received[q, :, pl.ds(first, UNIT_TERMS), :])
            return carry

        lax.fori_loop(0, self.units, combine_unit, 0)
        rows = self.units * UNIT
        first_row = pl.multiple_of((self.first_unit + q * self.units) * UNIT, UNIT)

        def add_blocks(i, carry):
            for j in range(8):
                b = i * 8 + j
                env.table[b, pl.ds(first_row, rows), :] += env.delta[env.slots[0, b], pl.ds(0, rows), :]
            return carry

        lax.fori_loop(0, BLOCKS // 8, add_blocks, 0)

    def finish(self, q):
        def finish_unit(h, carry):
            self.env.finish_unit(self.first_unit + q * self.units + h)
            return carry

        lax.fori_loop(0, self.units, finish_unit, 0)

    def at(self, s, do):
        @pl.when((s >= self.first_chunk) & (s < self.first_chunk + self.chunks))
        def _():
            do(s - self.first_chunk)

    def drain(self):
        def wait(q, carry):
            self.all_terms(q).wait_send()
            return carry

        lax.fori_loop(0, self.chunks, wait, 0)


class Env:
    def build_selector(self):
        ids = jnp.concatenate([self.id_recv[i] for i in range(PEERS)] + [self.id_send[PEERS]], axis=0)
        row_in_unit = lax.broadcasted_iota(jnp.int32, (OWNERS, E), 1) % UNIT
        keys = jnp.full((OWNERS, E), -1, jnp.int32)
        for b in range(BLOCKS):
            keys = jnp.where(ids == b, self.slots[0, b] * UNIT + row_in_unit, keys)
        lane = lax.broadcasted_iota(jnp.int32, (1, E), 1)
        per_tile = E // UNIT_TERMS
        lane_tiles = []
        for first in range(0, OWNERS, per_tile):
            tile = keys[first : first + 1, :]
            for j in range(1, per_tile):
                tile = jnp.where(lane >= j * UNIT_TERMS, keys[first + j : first + j + 1, :], tile)
            lane_tiles.append(jnp.broadcast_to(tile, (16, E)))
        row_index = lax.broadcasted_iota(jnp.int32, (16, E), 0)

        def selector_rows(p, carry):
            wanted = row_index + p * 16
            tiles = [jnp.where(tile == wanted, 1.0, 0.0).astype(jnp.bfloat16) for tile in lane_tiles]
            self.selector[pl.ds(pl.multiple_of(p * 16, 16), 16), :] = jnp.concatenate(tiles, axis=1)
            return carry

        lax.fori_loop(0, BLOCKS * UNIT // 16, selector_rows, 0)

    def combine_unit(self, unit, h, terms):
        block_rows = pl.ds(pl.multiple_of(unit * UNIT, UNIT), UNIT)
        delta_rows = pl.ds(pl.multiple_of(h * UNIT, UNIT), UNIT)
        terms = terms.reshape(OWNERS * UNIT_TERMS, E)
        sums = jnp.dot(self.selector[...], terms, preferred_element_type=jnp.float32)
        grad = sums.astype(jnp.bfloat16).astype(jnp.float32).reshape(BLOCKS, UNIT, E)
        mine = self.slot_lanes.reshape(1, 1, E) == lax.broadcasted_iota(jnp.int32, (BLOCKS, UNIT, E), 0)
        old = self.accum_t[block_rows, :] * float(E)
        accum = jnp.sum(jnp.where(mine, old[None], 0.0) + grad * grad, axis=-1, keepdims=True) * (1.0 / E)
        change = grad * (-LEARN_RATE * lax.rsqrt(accum))
        self.delta_send[unit] = change.astype(jnp.bfloat16).reshape(BLOCKS * UNIT, E)
        for step in range(1, CODERS):
            holder = (self.code + step) % CODERS
            span = pl.ds(pl.multiple_of(holder * (HELD * UNIT), HELD * UNIT), HELD * UNIT)
            pltpu.make_async_remote_copy(
                src_ref=self.delta_send.at[unit, span], dst_ref=self.delta_recv.at[unit, step - 1],
                send_sem=self.delta_send_sem.at[unit], recv_sem=self.delta_recv_sem.at[unit],
                device_id=(self.me, holder), device_id_type=MESH,
            ).start()
        self.delta[:, delta_rows, :] = change
        self.new_accum_t[block_rows, :] = jnp.sum(jnp.where(mine, accum, 0.0), axis=0)
        self.parity[:, block_rows, :] += self.delta[pl.ds(self.code * HELD, HELD), delta_rows, :]

    def all_deltas(self, unit):
        return pltpu.make_async_remote_copy(
            src_ref=self.delta_recv.at[unit], dst_ref=self.delta_recv.at[unit],
            send_sem=self.delta_send_sem.at[unit], recv_sem=self.delta_recv_sem.at[unit],
            device_id=(self.me, self.code), device_id_type=MESH,
        )

    def finish_unit(self, unit):
        block_rows = pl.ds(pl.multiple_of(unit * UNIT, UNIT), UNIT)
        self.all_deltas(unit).wait_recv()
        total = self.parity[:, block_rows, :]
        for j in range(CODERS - 1):
            total += self.delta_recv[unit, j].astype(jnp.float32).reshape(HELD, UNIT, E)
        self.parity[:, block_rows, :] = total

    def drain(self):
        def wait(unit, carry):
            self.all_deltas(unit).wait_send()
            return carry

        lax.fori_loop(0, UNITS, wait, 0)


def kernel(
    pooled_hbm, bags_hbm, dest_hbm, counts_hbm, table_hbm, accum_hbm, parity_hbm, slots_hbm,
    table, accum_out, parity,
    pooled, bags, dest, counts, slots, accum, id_send, id_recv, accum_t, new_accum_t,
    selector, delta, delta_send, delta_recv,
    in_sem, id_send_sem, id_recv_sem, delta_send_sem, delta_recv_sem, *stage_scratch,
):
    me = lax.axis_index("table")
    code = lax.axis_index("code")
    z, x, core = me // (RING * CORES), (me // CORES) % RING, me % CORES
    owners = [
        (((z + dz) % RING) * RING + (x + dx) % RING) * CORES + (core + dc) % CORES for dz, dx, dc in ORDER
    ] + [me]

    env = Env()
    env.me, env.code, env.owners = me, code, owners
    env.pooled, env.bags, env.counts, env.slots = pooled, bags, counts, slots
    env.id_send, env.id_recv, env.accum_t, env.new_accum_t = id_send, id_recv, accum_t, new_accum_t
    env.selector, env.delta, env.delta_send, env.delta_recv = selector, delta, delta_send, delta_recv
    env.delta_send_sem, env.delta_recv_sem = delta_send_sem, delta_recv_sem
    env.table, env.parity = table, parity
    half = len(stage_scratch) // 2
    wide = Stage(WIDE_UNITS, 0, 0, WIDE_CHUNKS, env, stage_scratch[:half])
    thin = Stage(THIN_UNITS, WIDE_UNITS * WIDE_CHUNKS, WIDE_CHUNKS, THIN_CHUNKS, env, stage_scratch[half:])
    stages = (wide, thin)

    sources = (counts_hbm, dest_hbm, slots_hbm, pooled_hbm, bags_hbm, accum_hbm, table_hbm, parity_hbm)
    places = (counts, dest, slots, pooled, bags, accum, table, parity)
    loads = [pltpu.make_async_copy(a, b, in_sem.at[i]) for i, (a, b) in enumerate(zip(sources, places))]
    for load in loads[:6]:
        load.start()

    barrier = pltpu.get_barrier_semaphore()
    for owner in owners[:PEERS]:
        pl.semaphore_signal(barrier, inc=1, device_id=(owner, code), device_id_type=MESH)
    for step in range(1, CODERS):
        pl.semaphore_signal(barrier, inc=1, device_id=(me, (code + step) % CODERS), device_id_type=MESH)

    for load in loads[:5]:
        load.wait()

    def send_ids():
        lane_slot = (lax.broadcasted_iota(jnp.int32, (1, E), 1) // UNIT) % CAP
        for i, owner in enumerate(owners):
            ids = jnp.full((1, E), -1, jnp.int32)
            for k in range(CAP):
                ids = jnp.where((lane_slot == k) & (k < counts[0, owner]), dest[k, owner], ids)
            id_send[i] = ids
        for i, owner in enumerate(owners[:PEERS]):
            pltpu.make_async_remote_copy(
                src_ref=id_send.at[i], dst_ref=id_recv.at[i], send_sem=id_send_sem, recv_sem=id_recv_sem,
                device_id=(owner, code), device_id_type=MESH,
            ).start()

    def all_ids():
        return pltpu.make_async_remote_copy(
            src_ref=id_send.at[pl.ds(0, PEERS)], dst_ref=id_recv, send_sem=id_send_sem, recv_sem=id_recv_sem,
            device_id=(me, code), device_id_type=MESH,
        )

    lane = lax.broadcasted_iota(jnp.int32, (1, E), 1)
    env.slot_lanes = jnp.full((1, E), -1, jnp.int32)
    for b in range(BLOCKS):
        env.slot_lanes = jnp.where(lane == b, slots[0, b], env.slot_lanes)

    def step(s, carry):
        def all_here():
            @pl.when(s == 0)
            def _():
                pl.semaphore_wait(barrier, PEERS + CODERS - 1)

        wide.at(s, lambda q: wide.send_terms(q, all_here))
        thin.at(s, thin.send_terms)

        @pl.when(s == 0)
        def _():
            send_ids()
            loads[6].start()
            loads[7].start()
            loads[5].wait()
            padding = jnp.zeros((BLK - BLOCKS, BLK), jnp.float32)
            accum_t[...] = jnp.concatenate([accum[...], padding], axis=0).T

        @pl.when(s == 1)
        def _():
            all_ids().wait_recv()
            env.build_selector()
            loads[6].wait()
            loads[7].wait()

        for stage in stages:
            stage.at(s - LAG, stage.combine)
        for stage in stages:
            stage.at(s - LAG - 2, stage.finish)
        return carry

    lax.fori_loop(0, WIDE_CHUNKS + THIN_CHUNKS + LAG + 2, step, 0)
    accum_out[...] = new_accum_t[...].T[:BLOCKS, :]
    all_ids().wait_send()
    env.drain()
    for stage in stages:
        stage.drain()


def body(pooled_grad, bag_rows, dest_blocks, block_counts, table, accum, parity, parity_slot):
    hbm = pl.BlockSpec(memory_space=pltpu.HBM)
    vmem = pl.BlockSpec(memory_space=pltpu.VMEM)
    dma = pltpu.SemaphoreType.DMA
    f32, bf16, i32 = jnp.float32, jnp.bfloat16, jnp.int32
    results = ((BLOCKS, BLK, E), (BLOCKS, BLK), (HELD, BLK, E))
    arrays = (
        pooled_grad[0, 0], bag_rows[0, 0], dest_blocks[0, 0].T, block_counts[0],
        table[0, 0], accum[0, 0], parity[0], parity_slot[0],
    )
    new_table, new_accum, new_parity = pl.pallas_call(
        kernel,
        name="adagrad_step",
        out_shape=[pltpu.VMEM(shape, f32) for shape in results],
        in_specs=[hbm] * len(arrays),
        out_specs=[vmem] * len(results),
        scratch_shapes=[
            pltpu.VMEM((BATCH, E), bf16),
            pltpu.VMEM((OWNERS, CAP, BATCH), i32),
            pltpu.SMEM((CAP, OWNERS), i32),
            pltpu.SMEM((1, OWNERS), i32),
            pltpu.SMEM((1, BLOCKS), i32),
            pltpu.VMEM((BLOCKS, BLK), f32),
            pltpu.VMEM((OWNERS, 1, E), i32),
            pltpu.VMEM((PEERS, 1, E), i32),
            pltpu.VMEM((BLK, BLK), f32),
            pltpu.VMEM((BLK, BLK), f32),
            pltpu.VMEM((BLOCKS * UNIT, OWNERS * UNIT_TERMS), bf16),
            pltpu.VMEM((BLOCKS, WIDE_UNITS * UNIT, E), f32),
            pltpu.VMEM((UNITS, BLOCKS * UNIT, E), bf16),
            pltpu.VMEM((UNITS, CODERS - 1, HELD * UNIT, E), bf16),
            dma((len(arrays),)),
            dma,
            dma,
            dma((UNITS,)),
            dma((UNITS,)),
            *Stage.scratch_shapes(WIDE_UNITS, WIDE_CHUNKS),
            *Stage.scratch_shapes(THIN_UNITS, THIN_CHUNKS),
        ],
        compiler_params=pltpu.CompilerParams(
            collective_id=0, has_side_effects=True, vmem_limit_bytes=40 * 1024 * 1024
        ),
    )(*[pltpu.with_memory_space_constraint(array, pltpu.HBM) for array in arrays])
    return (new_table[None, None], new_accum[None, None], new_parity[None])


def solution(mesh):
    placed = (
        P("table", "code", None, None),
        P("table", "code", None, None, None),
        P("table", "code", None, None),
        P("table", "code", None),
        P("table", "code", None, None, None),
        P("table", "code", None, None),
        P("table", "code", None, None),
        P("table", "code", None),
    )
    return jax.shard_map(
        body,
        mesh=mesh,
        in_specs=placed,
        out_specs=(
            P("table", "code", None, None, None),
            P("table", "code", None, None),
            P("table", "code", None, None),
        ),
        check_vma=False,
    )
```

time: 261 us -> 72.3 us (0.28)
  waiting for transfers between devices: 101 us -> 0 us
  Pallas kernels: 0 us -> 67 us
  matrix products: 53.5 us -> 0 us
  other arithmetic: 41.2 us -> 0 us
  local copies, waits for them, and re-layouts: 32.7 us -> 4.47 us
  starting transfers between devices: 17 us -> 0 us
  between operations: 14.2 us -> 0.64 us
    pallas_call x0 -> x1, Pallas kernels: none -> 67 us  [body(): pl.pallas_call(kernel, name='adagrad_step', out_shape=[pltpu.VMEM(shape,...]
    reduce_scatter x1 -> x0, waiting for transfers between devices: 54.3 us -> none  [body(): lax.psum_scatter(placed, 'code', scatter_dimension=0, tiled=True)]
    dot_general x17 -> x0, matrix products: 53.5 us -> none  [the longest x16 48.4 us: slot_terms(): jnp.einsum('grs,se->gre', onehot, pooled, preferred_element_type=jnp.floa...]
    all_to_all x2 -> x0, waiting for transfers between devices: 46.3 us -> none  [the longest x1 46.3 us: body(): lax.all_to_all(sent_rows, 'table', split_axis=0, concat_axis=0, tiled=True)]
    gather x33 -> x0, local copies, waits for them, and re-layouts: 26 us -> none  [the longest x16 10.4 us: slot_terms(): keep_mask = jnp.take(flat_live, indices, axis=0)]
    all_to_all x2 -> x0, starting transfers between devices: 17 us -> none  [the longest x1 9.43 us: body(): lax.all_to_all(marked, 'table', split_axis=0, concat_axis=0, tiled=True)]
    lt x16 -> x0, other arithmetic: 11.7 us -> none  [body(): lax.broadcasted_iota(jnp.int32, (owners, capacity), 1) < counts[:, None]]
    add x2 -> x0, other arithmetic: 9.67 us -> none  [the longest x1 9.04 us: body(): new_table = table[0, 0] + row_delta]
  transfers between devices with their start and end apart: 3 -> 0, of which waited for: 2 -> 0; matrix products, arithmetic and copies ran while one was open for 38% -> 0% of each run, Pallas kernels for 0% -> 0%
where the time goes in v2:
time: 72.3 us; the launch traced here: 72.1 us
  Pallas kernels  67 us (93%)
  local copies, waits for them, and re-layouts  4.47 us (6%)
    pallas_call x1, Pallas kernels, body(): pl.pallas_call(kernel, name='adagrad_step', out_shape=[pltpu.VMEM(shape,...  67 us
    unnamed x3, local copies, waits for them, and re-layouts  4.47 us

profile of v2, /device:TPU:1, one launch (start us, length us, event | category | flops | bytes accessed | tf_op | source)
XLA Modules:
  0.0 72.1 jit_solution(13577758817092773075)
XLA Ops:
  0.6 67.0 %adagrad_step.1 = (f32[96,128,128]{2,1,0:T(8,128)S(1)}, f32[96,128]{1,0:T(8,128)S(1)}, f32[24,128,128]{2,1,0:T(8,128)S(1)}) custom-call(bf16[2048,128]{1,0:T(8,128)(2,1)} %bitcast.19, s32[32,4,2048]{2,1,0:T(4,128)} %bitcast.18, s32[4,32]{1,0:T(4,128)} %bitcast.21, s32[1,32]{1,0:T(1,128)} %bitcast.22, f32[96,128,128]{2,1,0:T(8,128)} %bitcast.16, ...), custom_call_target="tpu_custom_call" | custom-call | tf_op jit(solution)/shard_map/adagrad_step/pallas_call | solution.py:331
  67.7 2.7 %copy.14 = f32[1,1,96,128,128]{4,3,2,1,0:T(8,128)} copy(f32[1,1,96,128,128]{4,3,2,1,0:T(8,128)S(1)} %bitcast.13) | data formatting | bytes 12582912
  70.4 0.6 copy.15
  71.0 1.1 %copy.16 = f32[1,24,128,128]{3,2,1,0:T(8,128)} copy(f32[1,24,128,128]{3,2,1,0:T(8,128)S(1)} %bitcast.14) | data formatting | bytes 3145728

commit v3 on v2

--- a/solution.py
+++ b/solution.py
@@ -24,6 +24,7 @@
 UNIT_TERMS = CAP * UNIT
 WIDE_UNITS, WIDE_CHUNKS = 2, 7
 THIN_UNITS, THIN_CHUNKS = 1, 2
+CHUNKS = WIDE_CHUNKS + THIN_CHUNKS
 DOT_ROWS = 512
 LAG = 2
 
@@ -41,12 +42,13 @@
 
 
 ORDER = send_order()
+BAG_PARTS = [pl.ds(0, OWNERS // 2), pl.ds(OWNERS // 2, OWNERS // 2)]
 PEERS = len(ORDER)
 
 
 class Stage:
-    def __init__(self, units, first_unit, first_chunk, chunks, env, scratch):
-        self.units, self.first_unit, self.first_chunk, self.chunks = units, first_unit, first_chunk, chunks
+    def __init__(self, units, chunks, unit_of, half_of, env, scratch):
+        self.units, self.chunks, self.unit_of, self.half_of = units, chunks, unit_of, half_of
         self.env = env
         self.sent, self.received, self.send_sem, self.recv_sem = scratch
 
@@ -63,7 +65,7 @@
     def send_terms(self, q, before_first_send=None):
         env = self.env
         terms = self.units * UNIT_TERMS
-        row_index = lax.broadcasted_iota(jnp.int32, (UNIT, E), 0) + (self.first_unit + q * self.units) * UNIT
+        row_index = lax.broadcasted_iota(jnp.int32, (UNIT, E), 0) + self.unit_of(q) * UNIT
         group = DOT_ROWS // terms
         for start in range(0, OWNERS, group):
             tiles, part = [], []
@@ -85,9 +87,16 @@
             else:
                 self.sent[q, pl.ds(start, group - 1)] = sums[: group - 1]
                 self.received[q, PEERS] = sums[group - 1]
-        if before_first_send is not None:
-            before_first_send()
-        for i in range(PEERS):
+            if self.units == THIN_UNITS:
+                self.send(q, start, start + group, before_first_send if start == 0 else None)
+        if self.units != THIN_UNITS:
+            self.send(q, 0, OWNERS, before_first_send)
+
+    def send(self, q, first, last, before):
+        env = self.env
+        if before is not None:
+            before()
+        for i in range(first, min(last, PEERS)):
             pltpu.make_async_remote_copy(
                 src_ref=self.sent.at[q, i], dst_ref=self.received.at[q, i],
                 send_sem=self.send_sem.at[q], recv_sem=self.recv_sem.at[q],
@@ -106,34 +115,33 @@
         self.all_terms(q).wait_recv()
 
         def combine_unit(h, carry):
-            unit = self.first_unit + q * self.units + h
+            unit = self.unit_of(q) + h
             first = pl.multiple_of(h * UNIT_TERMS, UNIT_TERMS)
-            env.combine_unit(unit, h, self.received[q, :, pl.ds(first, UNIT_TERMS), :])
+            env.combine_unit(unit, self.half_of(q), h, self.received[q, :, pl.ds(first, UNIT_TERMS), :])
             return carry
 
         lax.fori_loop(0, self.units, combine_unit, 0)
+
+    def add_blocks(self, q):
+        env = self.env
+        half = self.half_of(q)
         rows = self.units * UNIT
-        first_row = pl.multiple_of((self.first_unit + q * self.units) * UNIT, UNIT)
-
-        def add_blocks(i, carry):
+        first_row = pl.multiple_of(self.unit_of(q) * UNIT, UNIT)
+
+        def add_some(i, carry):
             for j in range(8):
                 b = i * 8 + j
-                env.table[b, pl.ds(first_row, rows), :] += env.delta[env.slots[0, b], pl.ds(0, rows), :]
-            return carry
-
-        lax.fori_loop(0, BLOCKS // 8, add_blocks, 0)
+                env.table[b, pl.ds(first_row, rows), :] += env.delta[half, env.slots[0, b], pl.ds(0, rows), :]
+            return carry
+
+        lax.fori_loop(0, BLOCKS // 8, add_some, 0)
 
     def finish(self, q):
         def finish_unit(h, carry):
-            self.env.finish_unit(self.first_unit + q * self.units + h)
+            self.env.finish_unit(self.unit_of(q) + h)
             return carry
 
         lax.fori_loop(0, self.units, finish_unit, 0)
-
-    def at(self, s, do):
-        @pl.when((s >= self.first_chunk) & (s < self.first_chunk + self.chunks))
-        def _():
-            do(s - self.first_chunk)
 
     def drain(self):
         def wait(q, carry):
@@ -168,13 +176,13 @@
 
         lax.fori_loop(0, BLOCKS * UNIT // 16, selector_rows, 0)
 
-    def combine_unit(self, unit, h, terms):
+    def combine_unit(self, unit, half, h, terms):
         block_rows = pl.ds(pl.multiple_of(unit * UNIT, UNIT), UNIT)
         delta_rows = pl.ds(pl.multiple_of(h * UNIT, UNIT), UNIT)
         terms = terms.reshape(OWNERS * UNIT_TERMS, E)
         sums = jnp.dot(self.selector[...], terms, preferred_element_type=jnp.float32)
         grad = sums.astype(jnp.bfloat16).astype(jnp.float32).reshape(BLOCKS, UNIT, E)
-        mine = self.slot_lanes.reshape(1, 1, E) == lax.broadcasted_iota(jnp.int32, (BLOCKS, UNIT, E), 0)
+        mine = self.slot_lanes[...].reshape(1, 1, E) == lax.broadcasted_iota(jnp.int32, (BLOCKS, UNIT, E), 0)
         old = self.accum_t[block_rows, :] * float(E)
         accum = jnp.sum(jnp.where(mine, old[None], 0.0) + grad * grad, axis=-1, keepdims=True) * (1.0 / E)
         change = grad * (-LEARN_RATE * lax.rsqrt(accum))
@@ -187,9 +195,9 @@
                 send_sem=self.delta_send_sem.at[unit], recv_sem=self.delta_recv_sem.at[unit],
                 device_id=(self.me, holder), device_id_type=MESH,
             ).start()
-        self.delta[:, delta_rows, :] = change
+        self.delta[half, :, delta_rows, :] = change
         self.new_accum_t[block_rows, :] = jnp.sum(jnp.where(mine, accum, 0.0), axis=0)
-        self.parity[:, block_rows, :] += self.delta[pl.ds(self.code * HELD, HELD), delta_rows, :]
+        self.parity[:, block_rows, :] += self.delta[half, pl.ds(self.code * HELD, HELD), delta_rows, :]
 
     def all_deltas(self, unit):
         return pltpu.make_async_remote_copy(
@@ -217,16 +225,24 @@
 def kernel(
     pooled_hbm, bags_hbm, dest_hbm, counts_hbm, table_hbm, accum_hbm, parity_hbm, slots_hbm,
     table, accum_out, parity,
-    pooled, bags, dest, counts, slots, accum, id_send, id_recv, accum_t, new_accum_t,
+    pooled, bags, dest, counts, slots, accum, id_send, id_recv, accum_t, new_accum_t, slot_lanes,
     selector, delta, delta_send, delta_recv,
     in_sem, id_send_sem, id_recv_sem, delta_send_sem, delta_recv_sem, *stage_scratch,
 ):
+    sources = (counts_hbm, pooled_hbm, *[bags_hbm.at[part] for part in BAG_PARTS], dest_hbm, slots_hbm, accum_hbm, table_hbm, parity_hbm)
+    places = (counts, pooled, *[bags.at[part] for part in BAG_PARTS], dest, slots, accum, table, parity)
+    loads = [pltpu.make_async_copy(a, b, in_sem.at[i]) for i, (a, b) in enumerate(zip(sources, places))]
+    first, second, last = loads[:-5], loads[-5:-2], loads[-2:]
+    for load in first + second:
+        load.start()
+
     me = lax.axis_index("table")
     code = lax.axis_index("code")
-    z, x, core = me // (RING * CORES), (me // CORES) % RING, me % CORES
-    owners = [
-        (((z + dz) % RING) * RING + (x + dx) % RING) * CORES + (core + dc) % CORES for dz, dx, dc in ORDER
-    ] + [me]
+    z, x, core = lax.div(me, RING * CORES), lax.rem(lax.div(me, CORES), RING), lax.rem(me, CORES)
+    zs = [lax.rem(z + d, RING) * (RING * CORES) for d in range(RING)]
+    xs = [lax.rem(x + d, RING) * CORES for d in range(RING)]
+    cores = [core, 1 - core]
+    owners = [zs[dz] + xs[dx] + cores[dc] for dz, dx, dc in ORDER] + [me]
 
     env = Env()
     env.me, env.code, env.owners = me, code, owners
@@ -234,17 +250,20 @@
     env.id_send, env.id_recv, env.accum_t, env.new_accum_t = id_send, id_recv, accum_t, new_accum_t
     env.selector, env.delta, env.delta_send, env.delta_recv = selector, delta, delta_send, delta_recv
     env.delta_send_sem, env.delta_recv_sem = delta_send_sem, delta_recv_sem
-    env.table, env.parity = table, parity
+    env.table, env.parity, env.slot_lanes = table, parity, slot_lanes
     half = len(stage_scratch) // 2
-    wide = Stage(WIDE_UNITS, 0, 0, WIDE_CHUNKS, env, stage_scratch[:half])
-    thin = Stage(THIN_UNITS, WIDE_UNITS * WIDE_CHUNKS, WIDE_CHUNKS, THIN_CHUNKS, env, stage_scratch[half:])
-    stages = (wide, thin)
-
-    sources = (counts_hbm, dest_hbm, slots_hbm, pooled_hbm, bags_hbm, accum_hbm, table_hbm, parity_hbm)
-    places = (counts, dest, slots, pooled, bags, accum, table, parity)
-    loads = [pltpu.make_async_copy(a, b, in_sem.at[i]) for i, (a, b) in enumerate(zip(sources, places))]
-    for load in loads[:6]:
-        load.start()
+    wide = Stage(WIDE_UNITS, WIDE_CHUNKS, lambda q: THIN_UNITS + q * WIDE_UNITS, lambda q: lax.rem(q + 1, 2), env, stage_scratch[:half])
+    thin = Stage(THIN_UNITS, THIN_CHUNKS, lambda q: q * (UNITS - THIN_UNITS), lambda q: 0, env, stage_scratch[half:])
+
+    def at_chunk(s, do):
+        @pl.when((s == 0) | (s == CHUNKS - 1))
+        def _():
+            do(thin, s // (CHUNKS - 1))
+
+        @pl.when((s > 0) & (s < CHUNKS - 1))
+        def _():
+            do(wide, s - 1)
+
 
     barrier = pltpu.get_barrier_semaphore()
     for owner in owners[:PEERS]:
@@ -252,7 +271,7 @@
     for step in range(1, CODERS):
         pl.semaphore_signal(barrier, inc=1, device_id=(me, (code + step) % CODERS), device_id_type=MESH)
 
-    for load in loads[:5]:
+    for load in first:
         load.wait()
 
     def send_ids():
@@ -274,26 +293,26 @@
             device_id=(me, code), device_id_type=MESH,
         )
 
-    lane = lax.broadcasted_iota(jnp.int32, (1, E), 1)
-    env.slot_lanes = jnp.full((1, E), -1, jnp.int32)
-    for b in range(BLOCKS):
-        env.slot_lanes = jnp.where(lane == b, slots[0, b], env.slot_lanes)
-
     def step(s, carry):
         def all_here():
             @pl.when(s == 0)
             def _():
                 pl.semaphore_wait(barrier, PEERS + CODERS - 1)
 
-        wide.at(s, lambda q: wide.send_terms(q, all_here))
-        thin.at(s, thin.send_terms)
+        at_chunk(s, lambda stage, q: stage.send_terms(q, all_here if stage is thin else None))
 
         @pl.when(s == 0)
         def _():
+            for load in last:
+                load.start()
+            for load in second:
+                load.wait()
             send_ids()
-            loads[6].start()
-            loads[7].start()
-            loads[5].wait()
+            lane = lax.broadcasted_iota(jnp.int32, (1, E), 1)
+            lanes = jnp.full((1, E), -1, jnp.int32)
+            for b in range(BLOCKS):
+                lanes = jnp.where(lane == b, slots[0, b], lanes)
+            slot_lanes[...] = lanes
             padding = jnp.zeros((BLK - BLOCKS, BLK), jnp.float32)
             accum_t[...] = jnp.concatenate([accum[...], padding], axis=0).T
 
@@ -301,21 +320,31 @@
         def _():
             all_ids().wait_recv()
             env.build_selector()
-            loads[6].wait()
-            loads[7].wait()
-
-        for stage in stages:
-            stage.at(s - LAG, stage.combine)
-        for stage in stages:
-            stage.at(s - LAG - 2, stage.finish)
+            for load in last:
+                load.wait()
+
+        at_chunk(s - LAG, lambda stage, q: stage.combine(q))
+        at_chunk(s - LAG - 1, lambda stage, q: stage.add_blocks(q))
+        at_chunk(s - LAG - 2, lambda stage, q: stage.finish(q))
         return carry
 
-    lax.fori_loop(0, WIDE_CHUNKS + THIN_CHUNKS + LAG + 2, step, 0)
+    lax.fori_loop(0, CHUNKS + LAG + 1, step, 0)
     accum_out[...] = new_accum_t[...].T[:BLOCKS, :]
     all_ids().wait_send()
+    wide.drain()
+    thin.drain()
+    thin.finish(THIN_CHUNKS - 1)
     env.drain()
-    for stage in stages:
-        stage.drain()
+
+
+def store(table, accum, parity, table_out, accum_out, parity_out, sem):
+    parts = [(table, table_out, pl.ds(first, HELD)) for first in range(0, BLOCKS, HELD)]
+    parts += [(parity, parity_out, pl.ds(0, HELD)), (accum, accum_out, pl.ds(0, BLOCKS))]
+    copies = [pltpu.make_async_copy(a.at[part], b.at[part], sem.at[i]) for i, (a, b, part) in enumerate(parts)]
+    for copy in copies:
+        copy.start()
+    for copy in copies:
+        copy.wait()
 
 
 def body(pooled_grad, bag_rows, dest_blocks, block_counts, table, accum, parity, parity_slot):
@@ -328,7 +357,7 @@
         pooled_grad[0, 0], bag_rows[0, 0], dest_blocks[0, 0].T, block_counts[0],
         table[0, 0], accum[0, 0], parity[0], parity_slot[0],
     )
-    new_table, new_accum, new_parity = pl.pallas_call(
+    updated = pl.pallas_call(
         kernel,
         name="adagrad_step",
         out_shape=[pltpu.VMEM(shape, f32) for shape in results],
@@ -345,11 +374,12 @@
             pltpu.VMEM((PEERS, 1, E), i32),
             pltpu.VMEM((BLK, BLK), f32),
             pltpu.VMEM((BLK, BLK), f32),
+            pltpu.VMEM((1, E), i32),
             pltpu.VMEM((BLOCKS * UNIT, OWNERS * UNIT_TERMS), bf16),
-            pltpu.VMEM((BLOCKS, WIDE_UNITS * UNIT, E), f32),
+            pltpu.VMEM((2, BLOCKS, WIDE_UNITS * UNIT, E), f32),
             pltpu.VMEM((UNITS, BLOCKS * UNIT, E), bf16),
             pltpu.VMEM((UNITS, CODERS - 1, HELD * UNIT, E), bf16),
-            dma((len(arrays),)),
+            dma((len(arrays) - 1 + len(BAG_PARTS),)),
             dma,
             dma,
             dma((UNITS,)),
@@ -361,6 +391,15 @@
             collective_id=0, has_side_effects=True, vmem_limit_bytes=40 * 1024 * 1024
         ),
     )(*[pltpu.with_memory_space_constraint(array, pltpu.HBM) for array in arrays])
+    new_table, new_accum, new_parity = pl.pallas_call(
+        store,
+        name="store_results",
+        out_shape=[jax.ShapeDtypeStruct(shape, f32) for shape in results],
+        in_specs=[vmem] * len(results),
+        out_specs=[hbm] * len(results),
+        scratch_shapes=[dma((BLOCKS // HELD + 2,))],
+        compiler_params=pltpu.CompilerParams(vmem_limit_bytes=4 * 1024 * 1024),
+    )(*updated)
     return (new_table[None, None], new_accum[None, None], new_parity[None])
 
 

time: 72.3 us -> 69.5 us (0.961)
  local copies, waits for them, and re-layouts: 4.47 us -> 0 us
  Pallas kernels: 67 us -> 68 us
    unnamed x3 -> x0, local copies, waits for them, and re-layouts: 4.47 us -> none
    pallas_call x0 -> x1, Pallas kernels: none -> 3.23 us  [body(): pl.pallas_call(store, name='store_results', out_shape=[jax.ShapeDtypeStru...]
    pallas_call x1, Pallas kernels: 67 us -> 64.8 us  [body(): pl.pallas_call(kernel, name='adagrad_step', out_shape=[pltpu.VMEM(shape,...]
where the time goes in v3:
time: 69.5 us; the launch traced here: 68.7 us
  Pallas kernels  68 us (98%)
    pallas_call x1, Pallas kernels, body(): pl.pallas_call(kernel, name='adagrad_step', out_shape=[pltpu.VMEM(shape,...  64.8 us
    pallas_call x1, Pallas kernels, body(): pl.pallas_call(store, name='store_results', out_shape=[jax.ShapeDtypeStru...  3.23 us

profile of v3, /device:TPU:1, one launch (start us, length us, event | category | flops | bytes accessed | tf_op | source)
XLA Modules:
  0.0 68.7 jit_solution(11016391944222023096)
XLA Ops:
  0.6 64.8 %adagrad_step.1 = (f32[96,128,128]{2,1,0:T(8,128)S(1)}, f32[96,128]{1,0:T(8,128)S(1)}, f32[24,128,128]{2,1,0:T(8,128)S(1)}) custom-call(bf16[2048,128]{1,0:T(8,128)(2,1)} %bitcast.16, s32[32,4,2048]{2,1,0:T(4,128)} %bitcast.15, s32[4,32]{1,0:T(4,128)} %bitcast.18, s32[1,32]{1,0:T(1,128)} %bitcast.19, f32[96,128,128]{2,1,0:T(8,128)} %bitcast.13, ...), custom_call_target="tpu_custom_call" | custom-call | tf_op jit(solution)/shard_map/adagrad_step/pallas_call | solution.py:360
  65.4 3.2 %store_results.1 = (f32[96,128,128]{2,1,0:T(8,128)}, f32[96,128]{1,0:T(8,128)}, f32[24,128,128]{2,1,0:T(8,128)}) custom-call(f32[96,128,128]{2,1,0:T(8,128)S(1)} %get-tuple-element.9.table, f32[96,128]{1,0:T(8,128)S(1)} %get-tuple-element.10.accum, f32[24,128,128]{2,1,0:T(8,128)S(1)} %get-tuple-element.11.parity), custom_call_target="tpu_custom_call" | custom-call | tf_op jit(solution)/shard_map/store_results/pallas_call | solution.py:394

commit v4 on v3

--- a/solution.py
+++ b/solution.py
@@ -180,24 +180,36 @@
         block_rows = pl.ds(pl.multiple_of(unit * UNIT, UNIT), UNIT)
         delta_rows = pl.ds(pl.multiple_of(h * UNIT, UNIT), UNIT)
         terms = terms.reshape(OWNERS * UNIT_TERMS, E)
-        sums = jnp.dot(self.selector[...], terms, preferred_element_type=jnp.float32)
-        grad = sums.astype(jnp.bfloat16).astype(jnp.float32).reshape(BLOCKS, UNIT, E)
-        mine = self.slot_lanes[...].reshape(1, 1, E) == lax.broadcasted_iota(jnp.int32, (BLOCKS, UNIT, E), 0)
         old = self.accum_t[block_rows, :] * float(E)
-        accum = jnp.sum(jnp.where(mine, old[None], 0.0) + grad * grad, axis=-1, keepdims=True) * (1.0 / E)
-        change = grad * (-LEARN_RATE * lax.rsqrt(accum))
-        self.delta_send[unit] = change.astype(jnp.bfloat16).reshape(BLOCKS * UNIT, E)
-        for step in range(1, CODERS):
-            holder = (self.code + step) % CODERS
-            span = pl.ds(pl.multiple_of(holder * (HELD * UNIT), HELD * UNIT), HELD * UNIT)
-            pltpu.make_async_remote_copy(
-                src_ref=self.delta_send.at[unit, span], dst_ref=self.delta_recv.at[unit, step - 1],
-                send_sem=self.delta_send_sem.at[unit], recv_sem=self.delta_recv_sem.at[unit],
-                device_id=(self.me, holder), device_id_type=MESH,
-            ).start()
-        self.delta[half, :, delta_rows, :] = change
-        self.new_accum_t[block_rows, :] = jnp.sum(jnp.where(mine, accum, 0.0), axis=0)
-        self.parity[:, block_rows, :] += self.delta[half, pl.ds(self.code * HELD, HELD), delta_rows, :]
+        held_rows = HELD * UNIT
+        new_accum = jnp.zeros((UNIT, E), jnp.float32)
+        for steps in ((2, 1), (3, 0)):
+            copies = []
+            for step in steps:
+                holder = lax.rem(self.code + step, CODERS)
+                span = pl.ds(pl.multiple_of(holder * held_rows, held_rows), held_rows)
+                sums = jnp.dot(self.selector[span, :], terms, preferred_element_type=jnp.float32)
+                grad = sums.astype(jnp.bfloat16).astype(jnp.float32).reshape(HELD, UNIT, E)
+                block = lax.broadcasted_iota(jnp.int32, (HELD, UNIT, E), 0) + holder * HELD
+                mine = self.slot_lanes[...].reshape(1, 1, E) == block
+                accum = jnp.sum(jnp.where(mine, old[None], 0.0) + grad * grad, axis=-1, keepdims=True) * (1.0 / E)
+                change = grad * (-LEARN_RATE * lax.rsqrt(accum))
+                new_accum += jnp.sum(jnp.where(mine, accum, 0.0), axis=0)
+                self.delta[half, pl.ds(holder * HELD, HELD), delta_rows, :] = change
+                if step == 0:
+                    self.parity[:, block_rows, :] += change
+                else:
+                    self.delta_send[unit, span, :] = change.astype(jnp.bfloat16).reshape(held_rows, E)
+                    copies.append(
+                        pltpu.make_async_remote_copy(
+                            src_ref=self.delta_send.at[unit, span], dst_ref=self.delta_recv.at[unit, step - 1],
+                            send_sem=self.delta_send_sem.at[unit], recv_sem=self.delta_recv_sem.at[unit],
+                            device_id=(self.me, holder), device_id_type=MESH,
+                        )
+                    )
+            for copy in copies:
+                copy.start()
+        self.new_accum_t[block_rows, :] = new_accum
 
     def all_deltas(self, unit):
         return pltpu.make_async_remote_copy(
@@ -219,7 +231,7 @@
             self.all_deltas(unit).wait_send()
             return carry
 
-        lax.fori_loop(0, UNITS, wait, 0)
+        lax.fori_loop(0, UNITS - 1, wait, 0)
 
 
 def kernel(
@@ -333,8 +345,9 @@
     all_ids().wait_send()
     wide.drain()
     thin.drain()
+    env.drain()
     thin.finish(THIN_CHUNKS - 1)
-    env.drain()
+    env.all_deltas(UNITS - 1).wait_send()
 
 
 def store(table, accum, parity, table_out, accum_out, parity_out, sem):

time: 69.5 us -> 68.4 us (0.984)
  Pallas kernels: 68 us -> 67.2 us
    pallas_call x1, Pallas kernels: 64.8 us -> 64 us  [body(): pl.pallas_call(kernel, name='adagrad_step', out_shape=[pltpu.VMEM(shape,...]
where the time goes in v4:
time: 68.4 us; the launch traced here: 67.8 us
  Pallas kernels  67.2 us (98%)
    pallas_call x1, Pallas kernels, body(): pl.pallas_call(kernel, name='adagrad_step', out_shape=[pltpu.VMEM(shape,...  64 us
    pallas_call x1, Pallas kernels, body(): pl.pallas_call(store, name='store_results', out_shape=[jax.ShapeDtypeStru...  3.23 us

profile of v4, /device:TPU:1, one launch (start us, length us, event | category | flops | bytes accessed | tf_op | source)
XLA Modules:
  0.0 67.8 jit_solution(8816288569817685107)
XLA Ops:
  0.6 64.0 %adagrad_step.1 = (f32[96,128,128]{2,1,0:T(8,128)S(1)}, f32[96,128]{1,0:T(8,128)S(1)}, f32[24,128,128]{2,1,0:T(8,128)S(1)}) custom-call(bf16[2048,128]{1,0:T(8,128)(2,1)} %bitcast.16, s32[32,4,2048]{2,1,0:T(4,128)} %bitcast.15, s32[4,32]{1,0:T(4,128)} %bitcast.18, s32[1,32]{1,0:T(1,128)} %bitcast.19, f32[96,128,128]{2,1,0:T(8,128)} %bitcast.13, ...), custom_call_target="tpu_custom_call" | custom-call | tf_op jit(solution)/shard_map/adagrad_step/pallas_call | solution.py:373
  64.6 3.2 %store_results.1 = (f32[96,128,128]{2,1,0:T(8,128)}, f32[96,128]{1,0:T(8,128)}, f32[24,128,128]{2,1,0:T(8,128)}) custom-call(f32[96,128,128]{2,1,0:T(8,128)S(1)} %get-tuple-element.9.table, f32[96,128]{1,0:T(8,128)S(1)} %get-tuple-element.10.accum, f32[24,128,128]{2,1,0:T(8,128)S(1)} %get-tuple-element.11.parity), custom_call_target="tpu_custom_call" | custom-call | tf_op jit(solution)/shard_map/store_results/pallas_call | solution.py:407

commit v5 on v4

--- a/solution.py
+++ b/solution.py
@@ -245,7 +245,7 @@
     places = (counts, pooled, *[bags.at[part] for part in BAG_PARTS], dest, slots, accum, table, parity)
     loads = [pltpu.make_async_copy(a, b, in_sem.at[i]) for i, (a, b) in enumerate(zip(sources, places))]
     first, second, last = loads[:-5], loads[-5:-2], loads[-2:]
-    for load in first + second:
+    for load in first:
         load.start()
 
     me = lax.axis_index("table")
@@ -283,6 +283,8 @@
     for step in range(1, CODERS):
         pl.semaphore_signal(barrier, inc=1, device_id=(me, (code + step) % CODERS), device_id_type=MESH)
 
+    for load in second:
+        load.start()
     for load in first:
         load.wait()
 
@@ -350,9 +352,13 @@
     env.all_deltas(UNITS - 1).wait_send()
 
 
+PIECE = 8
+
+
 def store(table, accum, parity, table_out, accum_out, parity_out, sem):
-    parts = [(table, table_out, pl.ds(first, HELD)) for first in range(0, BLOCKS, HELD)]
-    parts += [(parity, parity_out, pl.ds(0, HELD)), (accum, accum_out, pl.ds(0, BLOCKS))]
+    parts = [(accum, accum_out, pl.ds(0, BLOCKS))]
+    parts += [(parity, parity_out, pl.ds(first, PIECE)) for first in range(0, HELD, PIECE)]
+    parts += [(table, table_out, pl.ds(first, PIECE)) for first in range(0, BLOCKS, PIECE)]
     copies = [pltpu.make_async_copy(a.at[part], b.at[part], sem.at[i]) for i, (a, b, part) in enumerate(parts)]
     for copy in copies:
         copy.start()
@@ -410,7 +416,7 @@
         out_shape=[jax.ShapeDtypeStruct(shape, f32) for shape in results],
         in_specs=[vmem] * len(results),
         out_specs=[hbm] * len(results),
-        scratch_shapes=[dma((BLOCKS // HELD + 2,))],
+        scratch_shapes=[dma(((BLOCKS + HELD) // PIECE + 1,))],
         compiler_params=pltpu.CompilerParams(vmem_limit_bytes=4 * 1024 * 1024),
     )(*updated)
     return (new_table[None, None], new_accum[None, None], new_parity[None])

time: 68.4 us -> 68.4 us (level)
  no operation moved by 1% of the time
where the time goes in v5:
time: 68.4 us; the launch traced here: 67.9 us
  Pallas kernels  67.2 us (98%)
    pallas_call x1, Pallas kernels, body(): pl.pallas_call(kernel, name='adagrad_step', out_shape=[pltpu.VMEM(shape,...  64 us
    pallas_call x1, Pallas kernels, body(): pl.pallas_call(store, name='store_results', out_shape=[jax.ShapeDtypeStru...  3.28 us

profile of v5, /device:TPU:1, one launch (start us, length us, event | category | flops | bytes accessed | tf_op | source)
XLA Modules:
  0.0 67.9 jit_solution(6292642190706215352)
XLA Ops:
  0.6 64.0 %adagrad_step.1 = (f32[96,128,128]{2,1,0:T(8,128)S(1)}, f32[96,128]{1,0:T(8,128)S(1)}, f32[24,128,128]{2,1,0:T(8,128)S(1)}) custom-call(bf16[2048,128]{1,0:T(8,128)(2,1)} %bitcast.16, s32[32,4,2048]{2,1,0:T(4,128)} %bitcast.15, s32[4,32]{1,0:T(4,128)} %bitcast.18, s32[1,32]{1,0:T(1,128)} %bitcast.19, f32[96,128,128]{2,1,0:T(8,128)} %bitcast.13, ...), custom_call_target="tpu_custom_call" | custom-call | tf_op jit(solution)/shard_map/adagrad_step/pallas_call | solution.py:379
  64.6 3.3 %store_results.1 = (f32[96,128,128]{2,1,0:T(8,128)}, f32[96,128]{1,0:T(8,128)}, f32[24,128,128]{2,1,0:T(8,128)}) custom-call(f32[96,128,128]{2,1,0:T(8,128)S(1)} %get-tuple-element.9.table, f32[96,128]{1,0:T(8,128)S(1)} %get-tuple-element.10.accum, f32[24,128,128]{2,1,0:T(8,128)S(1)} %get-tuple-element.11.parity), custom_call_target="tpu_custom_call" | custom-call | tf_op jit(solution)/shard_map/store_results/pallas_call | solution.py:413
